TPU v7x, 32 devices: a whole 2x2x4 slice. The times are simulated.
32 devices in a mesh: dp: 4 (over z), cp: 8 (over y, x, core).
Axes of the slice: x: 2, y: 2, z: 4, core: 2. Of those that a mesh axis runs over, the one named last changes fastest.
Arguments:
- table_rows: bfloat16 [65536, 1024], P(('dp', 'cp')), may hold values from -6 to 6
- row_scales: float32 [65536], P(('dp', 'cp')), may hold values from 0.25 to 4
- owners: int32 [4096, 1], P(('dp', 'cp')), may hold values from 0 to 31; in each aligned block of 128 rows (0 to 127, 128 to 255, ...) at most 8 rows name the same one
- shard_rows: int32 [4096], P(('dp', 'cp')), may hold values from 0 to 2047
- history_lengths: int32 [4, 3], P('dp'), may hold values from 1 to 512, 1024 in all within a row
- input_weight: bfloat16 [1024, 4096], replicated, may hold values from -0.1875 to 0.1875
- output_weight: bfloat16 [1024, 1024], replicated, may hold values from -0.1875 to 0.1875
- cotangent: bfloat16 [4096, 1024], P(('dp', 'cp')), may hold values from -6 to 6
Outputs:
- layer_out: bfloat16 [4096, 1024], P(('dp', 'cp'))
- table_grad: float32 [65536, 1024], P(('dp', 'cp'))
Inputs may be any that keep to these rules, and one draw needn't show every extreme that they name: `owners`: among the events of one device no shard is named more than 8 times, and some device names one shard exactly 8 times. `history_lengths`: the 3 lengths of a cycle group sum to 1024; the longest is exactly 512.
All inputs are finite; a program needn't handle non-finite values.
Results may differ from a plain program's by a relative error of at most 0.0043.
Values may be sent and summed in bfloat16 or wider, within the bound.
A program may use at most 128 MiB of HBM per device.

v0:
```python
import jax
import jax.numpy as jnp
from jax import lax
from jax.sharding import PartitionSpec as P

HEADS = 8


EPSILON = 1e-05


def doc_bounds(lengths, positions):
    ends_at = jnp.cumsum(lengths)
    begins_at = ends_at - lengths
    inside = (positions[:, None] >= begins_at[None, :]) & (positions[:, None] < ends_at[None, :])
    doc_first = jnp.sum(jnp.where(inside, begins_at[None, :], 0), axis=1)
    doc_length = jnp.sum(jnp.where(inside, lengths[None, :], 0), axis=1).astype(jnp.float32)
    return (doc_first, doc_length)


def normalize(values):
    center = jnp.mean(values, axis=-1, keepdims=True)
    shifted = values - center
    inv_spread = lax.rsqrt(jnp.mean(shifted * shifted, axis=-1, keepdims=True) + EPSILON)
    return (shifted * inv_spread, inv_spread)


def normalize_back(grad_in, normed, inv_spread):
    return inv_spread * (
        grad_in
        - jnp.mean(grad_in, axis=-1, keepdims=True)
        - normed * jnp.mean(grad_in * normed, axis=-1, keepdims=True)
    )


def score_block(queries, key_block, query_pos, query_first, key_pos):
    scaling = queries.shape[-1] ** (-0.5)
    scores = (
        jnp.einsum("qhe,khe->hqk", queries, key_block, preferred_element_type=jnp.float32) * scaling
    )
    allowed = (key_pos[None, :] >= query_first[:, None]) & (key_pos[None, :] <= query_pos[:, None])
    return (scores, allowed[None])


def forward_part(queries, key_block, value_block, query_pos, query_first, query_length, key_pos):
    scores, allowed = score_block(queries, key_block, query_pos, query_first, key_pos)
    weights = jnp.where(
        allowed, scores * jax.nn.sigmoid(scores) / query_length[None, :, None], 0.0
    ).astype(jnp.bfloat16)
    return jnp.einsum("hqk,khe->qhe", weights, value_block, preferred_element_type=jnp.float32)


def backward_part(
    queries, key_block, value_block, grad_out, query_pos, query_first, query_length, key_pos
):
    scores, allowed = score_block(queries, key_block, query_pos, query_first, key_pos)
    sigmoid_part = jax.nn.sigmoid(scores)
    weights = jnp.where(allowed, scores * sigmoid_part / query_length[None, :, None], 0.0).astype(
        jnp.bfloat16
    )
    grad_weights = jnp.einsum(
        "qhe,khe->hqk", grad_out, value_block, preferred_element_type=jnp.float32
    )
    silu_slope = sigmoid_part * (1.0 + scores * (1.0 - sigmoid_part))
    scaling = queries.shape[-1] ** (-0.5)
    grad_scores = jnp.where(
        allowed, grad_weights * silu_slope / query_length[None, :, None] * scaling, 0.0
    ).astype(jnp.bfloat16)
    grad_query = jnp.einsum(
        "hqk,khe->qhe", grad_scores, key_block, preferred_element_type=jnp.float32
    )
    grad_key = jnp.einsum("hqk,qhe->khe", grad_scores, queries, preferred_element_type=jnp.float32)
    grad_value = jnp.einsum("hqk,qhe->khe", weights, grad_out, preferred_element_type=jnp.float32)
    return (grad_query, grad_key, grad_value)


def sweep(kernel, running, key_total, block_size, lowest, highest):

    def advance(block_index, current):
        block_start = block_index * block_size
        needed = (block_start <= highest) & (block_start + block_size > lowest)
        return lax.cond(
            needed,
            lambda state: kernel(state, block_start, block_size),
            lambda state: state,
            current,
        )

    return lax.fori_loop(0, key_total // block_size, advance, running)


def per_device(
    table_rows,
    row_scales,
    owners,
    shard_rows,
    history_lengths,
    input_weight,
    output_weight,
    cotangent,
):
    row_count = owners.shape[0]
    model_width = table_rows.shape[1]
    head_count = HEADS
    head_size = model_width // head_count
    devices = lax.axis_size(("dp", "cp"))
    capacity = max(2, 2 * row_count // devices)
    target = owners[:, 0]
    matches = (target[:, None] == jnp.arange(devices, dtype=jnp.int32)[None, :]).astype(jnp.int32)
    before = jnp.cumsum(matches, axis=0) - matches
    ranked = jnp.sum(before * matches, axis=1)
    placed = target * capacity + ranked
    requests = jnp.zeros((devices * capacity,), jnp.int32).at[placed].set(shard_rows + 1)
    incoming = lax.all_to_all(
        requests.reshape(devices, capacity), ("dp", "cp"), split_axis=0, concat_axis=0, tiled=True
    ).reshape(-1)
    wanted = incoming > 0
    lookup = jnp.maximum(incoming - 1, 0)
    fetched = jnp.where(
        wanted[:, None], table_rows[lookup].astype(jnp.float32) * row_scales[lookup][:, None], 0.0
    )
    returned = lax.all_to_all(
        fetched.reshape(devices, capacity, model_width),
        ("dp", "cp"),
        split_axis=0,
        concat_axis=0,
        tiled=True,
    )
    embedded = returned.reshape(devices * capacity, model_width)[placed]
    normed, inv_embed = normalize(embedded)
    projected = jnp.dot(
        normed.astype(jnp.bfloat16), input_weight, preferred_element_type=jnp.float32
    )
    activated = (projected * jax.nn.sigmoid(projected)).astype(jnp.bfloat16)
    gate_rows = activated[:, :model_width]
    value_rows = activated[:, model_width : 2 * model_width]
    query_rows = activated[:, 2 * model_width : 3 * model_width]
    key_rows = activated[:, 3 * model_width :]
    lengths = history_lengths[0]
    cycle_pos = lax.axis_index("cp") * row_count + jnp.arange(row_count, dtype=jnp.int32)
    query_first, query_length = doc_bounds(lengths, cycle_pos)
    lowest = jnp.min(query_first)
    highest = cycle_pos[row_count - 1]
    key_all, value_all = (
        lax.all_gather(key_rows, "cp", axis=0, tiled=True),
        lax.all_gather(value_rows, "cp", axis=0, tiled=True),
    )
    key_total = key_all.shape[0]
    queries = query_rows.reshape(row_count, head_count, head_size)

    def key_slices(block_start, piece_size):
        key_block = key_all.reshape(piece_size, head_count, head_size)
        value_block = value_all.reshape(piece_size, head_count, head_size)
        key_pos = block_start + jnp.arange(piece_size, dtype=jnp.int32)
        return (key_block, value_block, key_pos)

    def forward_kernel(running, block_start, piece_size):
        key_block, value_block, key_pos = key_slices(block_start, piece_size)
        return running + forward_part(
            queries, key_block, value_block, cycle_pos, query_first, query_length, key_pos
        )

    zeros_local = jnp.zeros((row_count, head_count, head_size), jnp.float32)
    attention = sweep(forward_kernel, zeros_local, key_total, key_total, lowest, highest).reshape(
        row_count, model_width
    )
    attn_norm, inv_attn = normalize(attention)
    mixed = attn_norm * gate_rows.astype(jnp.float32)
    output = embedded + jnp.dot(
        mixed.astype(jnp.bfloat16), output_weight, preferred_element_type=jnp.float32
    )
    layer_out = output.astype(jnp.bfloat16)
    grad_mixed = jnp.einsum(
        "rk,dk->rd", cotangent, output_weight, preferred_element_type=jnp.float32
    )
    grad_gate = grad_mixed * attn_norm
    grad_attn = normalize_back(
        grad_mixed * gate_rows.astype(jnp.float32), attn_norm, inv_attn
    ).astype(jnp.bfloat16)
    grad_heads = grad_attn.reshape(row_count, head_count, head_size)

    def query_kernel(running, block_start, piece_size):
        key_block, value_block, key_pos = key_slices(block_start, piece_size)
        return (
            running
            + backward_part(
                queries,
                key_block,
                value_block,
                grad_heads,
                cycle_pos,
                query_first,
                query_length,
                key_pos,
            )[0]
        )

    grad_query = sweep(query_kernel, zeros_local, key_total, key_total, lowest, highest)
    key_local = key_rows.reshape(row_count, head_count, head_size)
    value_local = value_rows.reshape(row_count, head_count, head_size)
    pieces = (
        lax.all_gather(query_rows, "cp", axis=0, tiled=True),
        lax.all_gather(grad_attn, "cp", axis=0, tiled=True),
    )
    piece_size = pieces[0].shape[0]
    positions = jnp.arange(piece_size, dtype=jnp.int32)
    piece_first, piece_length = doc_bounds(lengths, positions)
    partial_grads = backward_part(
        pieces[0].reshape(piece_size, head_count, head_size),
        key_local,
        value_local,
        pieces[1].reshape(piece_size, head_count, head_size),
        positions,
        piece_first,
        piece_length,
        cycle_pos,
    )
    grad_key = partial_grads[1]
    grad_value = partial_grads[2]
    grad_key = grad_key.reshape(row_count, model_width)
    grad_value = grad_value.reshape(row_count, model_width)
    grad_act = jnp.concatenate(
        [grad_gate, grad_value, grad_query.reshape(row_count, model_width), grad_key], axis=1
    )
    sigmoid_part = jax.nn.sigmoid(projected)
    grad_proj = (grad_act * sigmoid_part * (1.0 + projected * (1.0 - sigmoid_part))).astype(
        jnp.bfloat16
    )
    grad_norm = jnp.einsum("rk,dk->rd", grad_proj, input_weight, preferred_element_type=jnp.float32)
    grad_embed = cotangent.astype(jnp.float32) + normalize_back(grad_norm, normed, inv_embed)
    outgoing = jnp.zeros((devices * capacity, model_width), jnp.float32).at[placed].set(grad_embed)
    arrived = lax.all_to_all(
        outgoing.reshape(devices, capacity, model_width),
        ("dp", "cp"),
        split_axis=0,
        concat_axis=0,
        tiled=True,
    ).reshape(devices * capacity, model_width)
    summed = (
        jnp.zeros(table_rows.shape, jnp.float32)
        .at[lookup]
        .add(jnp.where(wanted[:, None], arrived, 0.0))
    )
    table_grad = summed * row_scales[:, None]
    return (layer_out, table_grad)


def solution(mesh):
    return jax.shard_map(
        per_device,
        mesh=mesh,
        in_specs=(
            P(("dp", "cp"), None),
            P(("dp", "cp")),
            P(("dp", "cp"), None),
            P(("dp", "cp")),
            P("dp", None),
            P(),
            P(),
            P(("dp", "cp"), None),
        ),
        out_specs=(P(("dp", "cp"), None), P(("dp", "cp"), None)),
        check_vma=False,
    )
```

profile of v0, /device:TPU:13, one launch (start us, length us, event | category | flops | bytes accessed | tf_op | source)
XLA Modules:
  0.0 266.3 jit_solution(5378104770503161528)
XLA Ops:
  11.5 10.8 %all_to_all.19 = s32[32,1,8]{2,1,0:T(1,128)S(1)} all-to-all(s32[32,1,8]{2,1,0:T(1,128)S(1)} %bitcast.157), channel_id=1, replica_groups=mesh['dp'=4,'cp'=8] {'dp','cp'}, dimensions={0} | all-to-all | bytes 2048 | tf_op jit(solution)/shard_map/all_to_all | solution.py:114
  24.7 4.3 %gather_fusion = bf16[256,1024]{1,0:T(8,128)(2,1)S(1)} fusion(bf16[2048,1024]{1,0:T(8,128)(2,1)} %param.12, s32[1024]{0:T(1024)S(1)} %pad_clamp_fusion.1), kind=kCustom, calls=%fused_computation | custom fusion | bytes 1049600 | tf_op jit(solution)/shard_map/gather | solution.py:120
  30.2 5.0 %all-to-all-start.1 = ((f32[32,8,1024]{2,1,0:T(8,128)}), f32[32,8,1024]{2,1,0:T(8,128)S(1)}, u32[]{:S(2)}, u32[]{:S(2)}) async-start(f32[32,8,1024]{2,1,0:T(8,128)} %fusion.49), calls=%async_computation.1 | async-start | bytes 2097152 | tf_op jit(solution)/shard_map/all_to_all | solution.py:122
  35.3 23.7 %all-to-all-done.1 = f32[32,8,1024]{2,1,0:T(8,128)S(1)} async-done(((f32[32,8,1024]{2,1,0:T(8,128)}), f32[32,8,1024]{2,1,0:T(8,128)S(1)}, u32[]{:S(2)}, u32[]{:S(2)}) %all-to-all-start.1) | async-done | bytes 1048608 | tf_op jit(solution)/shard_map/all_to_all | solution.py:122
  63.0 6.3 %multiply_convert_fusion = (bf16[128,4096]{1,0:T(8,128)(2,1)S(1)}, f32[128,4096]{1,0:T(8,128)}) fusion(bf16[1024,4096]{1,0:T(8,128)(2,1)} %param.17, f32[128,1024]{1,0:T(8,128)} %gather_fusion.2, f32[128]{0:T(128)S(1)} %add_rsqrt_fusion.1, f32[128]{0:T(128)S(1)} %broadcast_multiply_fusion.6), kind=kOutput, calls=%fused_computation.49 | convolution fusion | flops 1076756480 | bytes 12059648 | tf_op jit(solution)/shard_map/dot_general | solution.py:131
  78.2 22.6 %all-gather.7.cloned.1.call-done = bf16[1024,1024]{1,0:T(8,128)(2,1)} async-done(((bf16[128,1024]{1,0:T(8,128)(2,1)}), bf16[1024,1024]{1,0:T(8,128)(2,1)}) %all-gather.7.cloned.1.call-update) | async-done | bytes 2097168 | tf_op jit(solution)/shard_map/all_gather | solution.py:146
  100.8 29.8 %all-gather.5.cloned.1.call-done = bf16[1024,1024]{1,0:T(8,128)(2,1)} async-done(((bf16[128,1024]{1,0:T(8,128)(2,1)}), bf16[1024,1024]{1,0:T(8,128)(2,1)}) %all-gather.5.cloned.1.call-update) | async-done | bytes 2097168 | tf_op jit(solution)/shard_map/all_gather | solution.py:145
  130.6 6.7 %conditional.2 = (f32[128,8,128]{2,0,1:T(8,128)S(1)}) conditional(s32[]{:T(128)} %convert_element_type.66, (f32[128,8,128]{0,2,1:T(8,128)S(1)}) %tuple.51, (s32[128]{0:T(128)}, s32[128]{0:T(128)S(1)}, bf16[1024,1024]{1,0:T(8,128)(2,1)}, bf16[128,8,128]{2,1,0:T(8,128)(2,1)}, f32[128]{0:T(128)}, /*index=5*/bf16[1024,1024]{1,0:T(8,128)(2,1)}, ...), branch_computations={%region_9.10_spmd, %region_10.11_spmd} | conditional | flops 545783808 | bytes 6817288 | solution.py:82
  132.4 4.9 %fusion.8 = f32[128,8,128]{2,0,1:T(8,128)S(1)} fusion(f32[128,8,128]{2,0,1:T(8,128)} %copy.101, f32[128]{0:T(128)} %get-tuple-element.111, pred[128,1024]{1,0:T(8,128)(4,1)S(1)} %fusion.13, bf16[128,8,128]{2,1,0:T(8,128)(2,1)} %get-tuple-element.199, bf16[1024,1024]{1,0:T(8,128)(2,1)} %get-tuple-element.112, bf16[1024,1024]{1,0:T(8,128)(2,1)} %get-tuple-element.110), kind=kOutput, calls=%fused_computation.13 | convolution fusion | flops 545390592 | bytes 5636608 | tf_op jit(solution)/shard_map/while/body/eval_jaxpr/cond/branch_1_fun/hqk,khe->qhe/dot_general | solution.py:50
  142.6 19.2 %conditional.3 = (f32[128,1024]{1,0:T(8,128)}) conditional(s32[]{:T(128)} %convert_element_type.66, f32[128,8,128]{0,2,1:T(8,128)S(1)} %broadcast_in_dim.150, (s32[128]{0:T(128)}, s32[128]{0:T(128)S(1)}, bf16[128,1024]{1,0:T(8,128)(2,1)}, bf16[1024,1024]{1,0:T(8,128)(2,1)}, bf16[1024,1024]{1,0:T(8,128)(2,1)}, ...), branch_computations={%region_17.18_spmd, %region_18.19_spmd} | conditional | flops 819462144 | bytes 20710948 | solution.py:82
  144.3 4.0 %copy.108 = bf16[1024,1024]{0,1:T(8,128)(2,1)} copy(bf16[1024,1024]{1,0:T(8,128)(2,1)} %get-tuple-element.207) | data formatting | bytes 4194304 | tf_op jit(solution)/shard_map
  148.2 4.3 %fusion.19 = f32[8,128,1024]{2,1,0:T(8,128)} fusion(bf16[1024,1024]{1,0:T(8,128)(2,1)} %get-tuple-element.129, bf16[128,1024]{1,0:T(8,128)(2,1)S(1)} %copy-done.3), kind=kOutput, calls=%fused_computation.22 | convolution fusion | flops 268435456 | bytes 6553600 | tf_op jit(solution)/shard_map/while/body/eval_jaxpr/cond/branch_1_fun/qhe,khe->hqk/dot_general | solution.py:61
  152.6 7.2 %fusion.24 = f32[128,8,128]{0,2,1:T(8,128)} fusion(f32[128,8,128]{0,2,1:T(8,128)S(1)} %get-tuple-element.113, bf16[1024,8,128]{0,2,1:T(8,128)(2,1)} %bitcast.151, f32[8,128,1024]{2,1,0:T(8,128)} %fusion.19, f32[128]{0:T(128)} %get-tuple-element.132, pred[128,1024]{1,0:T(8,128)(4,1)} %fusion.25, bf16[128,8,128]{2,1,0:T(8,128)(2,1)} %get-tuple-element.208), kind=kOutput, calls=%fused_computation.27 | convolution fusion | flops 550633472 | bytes 7733760 | tf_op jit(solution)/shard_map/while/body/eval_jaxpr/cond/branch_1_fun/hqk,khe->qhe/dot_general | solution.py:69
  161.8 4.0 %copy.121 = bf16[1024,1024]{0,1:T(8,128)(2,1)} copy(bf16[1024,1024]{1,0:T(8,128)(2,1)} %all-gather.11.cloned.1.call-done) | data formatting | bytes 4194304 | tf_op jit(solution)/shard_map/reshape | solution.py:209
  165.8 4.4 %fusion.72 = f32[8,1024,128]{2,1,0:T(8,128)} fusion(bf16[1024,8,128]{0,2,1:T(8,128)(2,1)} %bitcast.147, bf16[16,8,8,128]{3,2,1,0:T(8,128)(2,1)S(1)} %copy-done.7), kind=kOutput, calls=%fused_computation.89 | convolution fusion | flops 268435456 | bytes 6553600 | tf_op jit(solution)/shard_map/qhe,khe->hqk/dot_general | solution.py:39
  170.3 19.8 %all-gather.9.cloned.1.call-done = bf16[1024,1024]{1,0:T(8,128)(2,1)} async-done(((bf16[128,1024]{1,0:T(8,128)(2,1)}), bf16[1024,1024]{1,0:T(8,128)(2,1)}) %all-gather.9.cloned.1.call-update) | async-done | bytes 2097168 | tf_op jit(solution)/shard_map/all_gather | solution.py:203
  190.1 4.9 %fusion.35 = f32[8,128,128]{2,1,0:T(8,128)S(1)} fusion(f32[8,1024,128]{2,1,0:T(8,128)} %fusion.72, f32[1024]{0:T(1024)S(1)} %copy-done.10, pred[1024,128]{1,0:T(8,128)(4,1)S(1)} %fusion.63, bf16[1024,1024]{1,0:T(8,128)(2,1)} %all-gather.9.cloned.1.call-done), kind=kOutput, calls=%fused_computation.43 | convolution fusion | flops 276824064 | bytes 6950912 | tf_op jit(solution)/shard_map/hqk,qhe->khe/dot_general | solution.py:73
  196.0 7.2 %fusion.44 = f32[8,128,128]{2,1,0:T(8,128)} fusion(bf16[1024,8,128]{0,2,1:T(8,128)(2,1)} %bitcast.148, f32[8,1024,128]{2,1,0:T(8,128)} %fusion.72, f32[1024]{0:T(1024)S(1)} %copy-done.10, pred[1024,128]{1,0:T(8,128)(4,1)S(1)} %fusion.63, bf16[16,8,8,128]{3,2,1,0:T(8,128)(2,1)S(1)} %copy-done.8, bf16[1024,1024]{1,0:T(8,128)(2,1)} %all-gather.9.cloned.1.call-done), kind=kOutput, calls=%fused_computation.54 | convolution fusion | flops 550502400 | bytes 9310208 | tf_op jit(solution)/shard_map/hqk,qhe->khe/dot_general | solution.py:72
  205.2 8.4 %fusion.99 = (f32[128]{0:T(128)S(1)}, f32[128]{0:T(128)S(1)}, f32[128,1024]{1,0:T(8,128)}) fusion(f32[128]{0:T(128)} %copy-done.19, f32[128,1024]{1,0:T(8,128)S(1)} %copy-done.2, f32[128]{0:T(128)} %copy-done.17, bf16[1024,4096]{1,0:T(8,128)(2,1)} %param.17, f32[128,1024]{1,0:T(8,128)} %copy.117, f32[128,1024]{1,0:T(8,128)} %get-tuple-element.213, ...), kind=kOutput, calls=%fused_computation.144 | convolution fusion | flops 1080688384 | bytes 13633536 | tf_op jit(solution)/shard_map/rk,dk->rd/dot_general | solution.py:229
  213.6 2.7 %scatter_custom_fusion.1 = f32[256,1024]{1,0:T(8,128)} fusion(s32[128]{0:T(128)} %copy-done.21, f32[128,1024]{1,0:T(8,128)} %get-tuple-element.233, bf16[128,1024]{1,0:T(8,128)(2,1)S(1)} %copy-done.6, f32[]{:T(128)} %constant.70.clone.1, f32[128,1024]{1,0:T(8,128)S(1)} %copy-done.2, f32[128]{0:T(128)S(1)} %broadcast_multiply_fusion.1, ...), kind=kCustom, calls=%fused_computation.67 | custom fusion | flops 1048576 | bytes 2361856 | tf_op jit(solution)/shard_map/scatter | solution.py:231
  216.3 4.9 %all-to-all-start.2 = ((f32[32,8,1024]{2,1,0:T(8,128)}), f32[32,8,1024]{2,1,0:T(8,128)}, u32[]{:S(2)}, u32[]{:S(2)}) async-start(f32[32,8,1024]{2,1,0:T(8,128)} %bitcast.150), calls=%async_computation.2 | async-start | bytes 2097152 | tf_op jit(solution)/shard_map/all_to_all | solution.py:232
  223.6 21.4 %all-to-all-done.2 = f32[32,8,1024]{2,1,0:T(8,128)} async-done(((f32[32,8,1024]{2,1,0:T(8,128)}), f32[32,8,1024]{2,1,0:T(8,128)}, u32[]{:S(2)}, u32[]{:S(2)}) %all-to-all-start.2) | async-done | bytes 1048608 | tf_op jit(solution)/shard_map/all_to_all | solution.py:232
  245.0 7.3 %scatter_custom_fusion.2 = f32[2048,1024]{1,0:T(8,128)} fusion(s32[256]{0:T(256)} %copy-done.9, f32[]{:T(128)} %constant.70.clone.1, f32[32,8,1024]{2,1,0:T(8,128)} %all-to-all-done.2, pred[256]{0:T(512)(128)(4,1)S(1)} %gt.23), kind=kCustom, calls=%fused_computation.41 | custom fusion | flops 524288 | bytes 9438464 | tf_op jit(solution)/shard_map/scatter-add | solution.py:242
  252.4 7.4 %broadcast_multiply_fusion = f32[2048,1024]{1,0:T(8,128)} fusion(f32[2048,1024]{1,0:T(8,128)} %scatter_custom_fusion.2, f32[2048]{0:T(1024)S(1)} %copy-done.1), kind=kLoop, calls=%fused_computation.37 | loop fusion | flops 2097152 | bytes 16785408 | tf_op jit(solution)/shard_map/mul | solution.py:244
  (108 shorter events, 35.4 us)
Async XLA Ops:
  7.2 130.5 %copy-start = (bf16[1024,1024]{1,0:T(8,128)(2,1)S(1)}, bf16[1024,1024]{1,0:T(8,128)(2,1)}, u32[]{:S(2)}) copy-start(bf16[1024,1024]{1,0:T(8,128)(2,1)} %param.18) | copy-start | bytes 6291460
  10.4 24.9 %copy-start.21 = (s32[128]{0:T(128)}, s32[128]{0:T(128)S(1)}, u32[]{:S(2)}) copy-start(s32[128]{0:T(128)S(1)} %fusion.85) | copy-start | bytes 1540
  30.2 28.8 %all-to-all-start.1 = ((f32[32,8,1024]{2,1,0:T(8,128)}), f32[32,8,1024]{2,1,0:T(8,128)S(1)}, u32[]{:S(2)}, u32[]{:S(2)}) async-start(f32[32,8,1024]{2,1,0:T(8,128)} %fusion.49), calls=%async_computation.1 | async-start | bytes 2097152 | tf_op jit(solution)/shard_map/all_to_all | solution.py:122
  35.2 65.6 %all-gather.7.cloned.1.call-start = ((), (), s32[]{:S(2)}) async-start(), calls=%async_computation.4 | async-start | bytes 2359296 | tf_op jit(solution)/shard_map/all_gather | solution.py:146
  61.7 7.6 %copy-start.17 = (f32[128]{0:T(128)}, f32[128]{0:T(128)S(1)}, u32[]{:S(2)}) copy-start(f32[128]{0:T(128)S(1)} %broadcast_multiply_fusion.6) | copy-start | bytes 1540
  63.0 6.3 %copy-start.19 = (f32[128]{0:T(128)}, f32[128]{0:T(128)S(1)}, u32[]{:S(2)}) copy-start(f32[128]{0:T(128)S(1)} %add_rsqrt_fusion.1) | copy-start | bytes 1540
  69.3 4.3 %copy-start.11 = (s32[1,3]{1,0:T(1,128)S(1)}, s32[1,3]{1,0:T(1,128)}, u32[]{:S(2)}) copy-start(s32[1,3]{1,0:T(1,128)} %param.16) | copy-start | bytes 40
  71.5 59.0 %all-gather.5.cloned.1.call-start = ((), (), s32[]{:S(2)}) async-start(), calls=%async_computation.3 | async-start | bytes 2359296 | tf_op jit(solution)/shard_map/all_gather | solution.py:145
  72.3 89.5 %all-gather.11.cloned.1.call-start = ((), (), s32[]{:S(2)}) async-start(), calls=%async_computation.6 | async-start | bytes 2359296 | tf_op jit(solution)/shard_map/all_gather | solution.py:202
  73.0 117.1 %all-gather.9.cloned.1.call-start = ((), (), s32[]{:S(2)}) async-start(), calls=%async_computation.5 | async-start | bytes 2359296 | tf_op jit(solution)/shard_map/all_gather | solution.py:203
  73.8 56.7 %copy-start.13 = (s32[3,1]{0,1:T(1,128)}, s32[3,1]{0,1:T(1,128)S(1)}, u32[]{:S(2)}) copy-start(s32[3,1]{0,1:T(1,128)S(1)} %reduce-window.4) | copy-start | bytes 40
  74.4 56.2 %copy-start.15 = (s32[3]{0:T(128)}, s32[3]{0:T(128)S(1)}, u32[]{:S(2)}) copy-start(s32[3]{0:T(128)S(1)} %fusion.86) | copy-start | bytes 40
  130.6 7.0 %copy-start.5 = (bf16[128,1024]{1,0:T(8,128)(2,1)S(1)}, bf16[128,1024]{1,0:T(8,128)(2,1)}, u32[]{:S(2)}) copy-start(bf16[128,1024]{1,0:T(8,128)(2,1)} %param.19) | copy-start | bytes 786436
  139.5 2.2 copy-start.12
  144.3 4.0 %copy-start.3 = (bf16[128,1024]{1,0:T(8,128)(2,1)S(1)}, bf16[128,1024]{1,0:T(8,128)(2,1)}, u32[]{:S(2)}) copy-start(bf16[128,1024]{1,0:T(8,128)(2,1)} %get-tuple-element.128) | copy-start | bytes 786436 | tf_op jit(solution)/shard_map/while/body/eval_jaxpr/cond
  161.8 4.0 %copy-start.7 = (bf16[16,8,8,128]{3,2,1,0:T(8,128)(2,1)S(1)}, bf16[16,8,8,128]{3,2,1,0:T(8,128)(2,1)}, u32[]{:S(2)}) copy-start(bf16[16,8,8,128]{3,2,1,0:T(8,128)(2,1)} %get-tuple-element.226) | copy-start | bytes 786436
  165.8 24.3 %copy-start.10 = (f32[1024]{0:T(1024)S(1)}, f32[1024]{0:T(1024)}, u32[]{:S(2)}) copy-start(f32[1024]{0:T(1024)} %convert_element_type.75) | copy-start | bytes 12292
  170.2 25.7 %copy-start.8 = (bf16[16,8,8,128]{3,2,1,0:T(8,128)(2,1)S(1)}, bf16[16,8,8,128]{3,2,1,0:T(8,128)(2,1)}, u32[]{:S(2)}) copy-start(bf16[16,8,8,128]{3,2,1,0:T(8,128)(2,1)} %get-tuple-element.224) | copy-start | bytes 786436
  196.0 9.2 %copy-start.2 = (f32[128,1024]{1,0:T(8,128)S(1)}, f32[128,1024]{1,0:T(8,128)}, u32[]{:S(2)}) copy-start(f32[128,1024]{1,0:T(8,128)} %gather_fusion.2) | copy-start | bytes 1572868
  205.2 8.4 %copy-start.6 = (bf16[128,1024]{1,0:T(8,128)(2,1)S(1)}, bf16[128,1024]{1,0:T(8,128)(2,1)}, u32[]{:S(2)}) copy-start(bf16[128,1024]{1,0:T(8,128)(2,1)} %param.19) | copy-start | bytes 786436
  205.2 8.4 %copy-start.18 = (f32[128]{0:T(128)S(1)}, f32[128]{0:T(128)}, u32[]{:S(2)}) copy-start(f32[128]{0:T(128)} %copy-done.17) | copy-start | bytes 1540
  205.2 8.4 %copy-start.20 = (f32[128]{0:T(128)S(1)}, f32[128]{0:T(128)}, u32[]{:S(2)}) copy-start(f32[128]{0:T(128)} %copy-done.19) | copy-start | bytes 1540
  216.3 28.7 %all-to-all-start.2 = ((f32[32,8,1024]{2,1,0:T(8,128)}), f32[32,8,1024]{2,1,0:T(8,128)}, u32[]{:S(2)}, u32[]{:S(2)}) async-start(f32[32,8,1024]{2,1,0:T(8,128)} %bitcast.150), calls=%async_computation.2 | async-start | bytes 2097152 | tf_op jit(solution)/shard_map/all_to_all | solution.py:232
  223.6 28.7 %copy-start.1 = (f32[2048]{0:T(1024)S(1)}, f32[2048]{0:T(1024)}, u32[]{:S(2)}) copy-start(f32[2048]{0:T(1024)} %param.13) | copy-start | bytes 24580
  (4 other events, 7.3 us)
Sparse Core Ops, SparseCore 0:
  71.7 29.0 all-gather.6
  102.7 27.8 all-gather.4
  132.5 27.8 all-gather.10
  162.2 27.8 all-gather.8
where the time goes:
time: 271 us; the launch traced here: 266 us
  waiting for transfers between devices  119 us (44%)
  matrix products  51.6 us (19%)
  other arithmetic  32.4 us (12%)
  local copies, waits for them, and re-layouts  27.2 us (10%)
  between operations  15.2 us (6%)
  blocking collectives  10.8 us (4%)
  starting transfers between devices  10.1 us (4%)
    all_gather x1, waiting for transfers between devices, per_device(): lax.all_gather(key_rows, 'cp', axis=0, tiled=True)  29.8 us
    all_to_all x1, waiting for transfers between devices, per_device(): lax.all_to_all(fetched.reshape(devices, capacity, model_width), ('dp', 'c...  23.7 us
    all_gather x1, waiting for transfers between devices, per_device(): lax.all_gather(value_rows, 'cp', axis=0, tiled=True)  22.6 us
    all_to_all x1, waiting for transfers between devices, per_device(): lax.all_to_all(outgoing.reshape(devices, capacity, model_width), ('dp', '...  21.4 us
    all_gather x1, waiting for transfers between devices, per_device(): lax.all_gather(grad_attn, 'cp', axis=0, tiled=True)  19.8 us
    all_to_all x1, blocking collectives, per_device(): lax.all_to_all(requests.reshape(devices, capacity), ('dp', 'cp'), split_a...  10.8 us
    dot_general x1, matrix products, per_device(): jnp.einsum('rk,dk->rd', grad_proj, input_weight, preferred_element_type=j...  8.38 us
    mul x1, other arithmetic, per_device(): table_grad = summed * row_scales[:, None]  7.39 us
  transfers between devices with their start and end apart: 6, of which 5 were waited for; matrix products, arithmetic and copies ran while one was open for 17% of the time, Pallas kernels for 0%

commit v1 on v0

v1 whole, which is shorter than its diff:
```python
import functools

import jax
import jax.numpy as jnp
from jax import lax
from jax.experimental import pallas as pl
from jax.experimental.pallas import tpu as pltpu
from jax.sharding import PartitionSpec as P

HEADS = 8
EPSILON = 1e-05
LANES = 128
MESH = pl.DeviceIdType.MESH
EXACT = lax.Precision.HIGHEST
F32 = jnp.float32
BF16 = jnp.bfloat16
VMEM_LIMIT = 60 * 1024 * 1024


def iota(shape, axis):
    return lax.broadcasted_iota(jnp.int32, shape, axis)


def dot_f32(a, b):
    return jnp.dot(a, b, precision=EXACT, preferred_element_type=F32)


def dot(a, b):
    return jnp.dot(a, b, preferred_element_type=F32)


def dot_nt(a, b):
    return lax.dot_general(a, b, (((1,), (1,)), ((), ())), preferred_element_type=F32)


def dot_tn(a, b):
    return lax.dot_general(a, b, (((0,), (0,)), ((), ())), preferred_element_type=F32)


def normalize(values):
    center = jnp.mean(values, axis=-1, keepdims=True)
    shifted = values - center
    inv_spread = lax.rsqrt(jnp.mean(shifted * shifted, axis=-1, keepdims=True) + EPSILON)
    return shifted * inv_spread, inv_spread


def normalize_back(grad_in, normed, inv_spread):
    return inv_spread * (
        grad_in
        - jnp.mean(grad_in, axis=-1, keepdims=True)
        - normed * jnp.mean(grad_in * normed, axis=-1, keepdims=True)
    )


def ranks_column(owner_col, devices):
    rows = owner_col.shape[0]
    match = (owner_col == iota((rows, devices), 1)).astype(F32)
    earlier = (iota((rows, rows), 1) < iota((rows, rows), 0)).astype(BF16)
    before = dot(earlier, match.astype(BF16))
    return jnp.sum(before * match, axis=1, keepdims=True).astype(jnp.int32)


def ranks_row(owner_row, devices):
    rows = owner_row.shape[1]
    match = (owner_row == iota((devices, rows), 0)).astype(F32)
    earlier = (iota((rows, rows), 0) < iota((rows, rows), 1)).astype(BF16)
    before = dot(match.astype(BF16), earlier)
    return jnp.sum(before * match, axis=0, keepdims=True).astype(jnp.int32)


def flat_index():
    return lax.axis_index("dp") * lax.axis_size("cp") + lax.axis_index("cp")


def flat_id(peer):
    size = lax.axis_size("cp")
    return {"dp": lax.div(peer, size), "cp": lax.rem(peer, size)}


def greet(me, count, to_id):
    barrier = pltpu.get_barrier_semaphore()

    @pl.loop(1, count)
    def _(k):
        pl.semaphore_signal(
            barrier, inc=1, device_id=to_id(lax.rem(me + k, count)), device_id_type=MESH
        )

    pl.semaphore_wait(barrier, count - 1)


def fetch_kernel(
    devices, capacity, own_col, own_row, row_col, table_any, scale_ref,
    incoming, got, got_scale,
    request, table, rows_out, scale_out, send_sem, recv_sem, local_sem,
):
    me = flat_index()
    slots = devices * capacity
    load = pltpu.make_async_copy(table_any, table, local_sem.at[0])
    load.start()
    rows = own_col.shape[0]
    rank = ranks_column(own_col[...], devices)
    spread = (rank == iota((rows, LANES), 1)).astype(F32) * (row_col[...] + 1).astype(F32)
    match = (own_row[...] == iota((devices, rows), 0)).astype(F32)
    wanted = (dot_f32(match, spread) + 0.5).astype(jnp.int32)
    for t in range(devices):
        request[t] = wanted[t : t + 1, :]
    greet(me, devices, flat_id)

    def link(kind, src, dst, peer, at_dst, sem):
        return pltpu.make_async_remote_copy(
            src_ref=src.at[peer],
            dst_ref=dst.at[at_dst],
            send_sem=send_sem.at[kind, peer],
            recv_sem=recv_sem.at[kind, sem],
            device_id=flat_id(peer),
            device_id_type=MESH,
        )

    def start(kind, src, dst):
        @pl.loop(1, devices)
        def _(k):
            link(kind, src, dst, lax.rem(me + k, devices), me, me).start()

    def arrive(kind, src, dst):
        @pl.loop(1, devices)
        def _(k):
            peer = lax.rem(me + k, devices)
            link(kind, src, dst, peer, peer, peer).wait_recv()

    def sent(kind, src, dst):
        @pl.loop(1, devices)
        def _(k):
            link(kind, src, dst, lax.rem(me + k, devices), me, me).wait_send()

    start(0, request, incoming)
    incoming[me] = request[me]
    load.wait()
    arrive(0, request, incoming)
    asked = incoming[:, 0, :].astype(F32)
    of_slot = (lax.div(iota((slots, devices), 0), capacity) == iota((slots, devices), 1)).astype(F32)
    lane_of = (lax.rem(iota((slots, LANES), 0), capacity) == iota((slots, LANES), 1)).astype(F32)
    index = (jnp.sum(dot_f32(of_slot, asked) * lane_of, axis=1, keepdims=True) + 0.5).astype(
        jnp.int32
    ) - 1
    total = table.shape[0]
    groups = total // LANES
    high = (lax.shift_right_arithmetic(index, 7) == iota((slots, groups), 1)).astype(F32)
    low = ((index & (LANES - 1)) == iota((slots, LANES), 1)).astype(F32)
    picked = jnp.sum(dot_f32(high, scale_ref[...]) * low, axis=1, keepdims=True)
    to_device = (
        lax.div(iota((devices, slots), 1), capacity) == iota((devices, slots), 0)
    ).astype(F32)
    scales = dot_f32(to_device, picked * lane_of)
    for t in range(devices):
        scale_out[t] = scales[t : t + 1, :]
    start(1, scale_out, got_scale)
    got_scale[me] = scale_out[me]
    one_hot = (index == iota((slots, total), 1)).astype(F32).astype(BF16)
    values = dot(one_hot, table[...])
    for t in range(devices):
        rows_out[t] = values[t * capacity : (t + 1) * capacity, :].astype(BF16)
    start(2, rows_out, got)
    got[me] = rows_out[me]
    arrive(1, scale_out, got_scale)
    arrive(2, rows_out, got)
    sent(0, request, incoming)
    sent(1, scale_out, got_scale)
    sent(2, rows_out, got)


def layer_kernel(
    devices, capacity, cp, lengths, own_col, own_row, got, got_scale, win_any, wout_any, cot_ref,
    layer_out, outgoing,
    win, wout, flat, slots_f32, projected, embedded, normed, gate_s, gm_s,
    snd_k, snd_v, snd_q, all_k, all_v, all_q,
    snd_att, all_att, snd_ga, all_ga, snd_dq, snd_dk, snd_dv, all_dq, all_dk, all_dv,
    weights, slope, dk_sum, dv_sum, gp_s,
    send_sem, recv_sem, local_sem,
):
    me = lax.axis_index("cp")
    rows, width = layer_out.shape
    heads = HEADS
    hd = width // heads
    share = cp // heads
    slots = devices * capacity
    mine = lax.rem(me, share)
    load_in = pltpu.make_async_copy(win_any, win, local_sem.at[0])
    load_out = pltpu.make_async_copy(wout_any, wout, local_sem.at[1])
    load_in.start()
    load_out.start()
    greet(me, cp, lambda peer: {"cp": peer})

    def link(kind, src, dst, peer, send_at, recv_at):
        return pltpu.make_async_remote_copy(
            src_ref=src,
            dst_ref=dst,
            send_sem=send_sem.at[kind, send_at],
            recv_sem=recv_sem.at[kind, recv_at],
            device_id={"cp": peer},
            device_id_type=MESH,
        )

    def spread(kind, src, dst, which):
        @pl.loop(1, cp)
        def _(k):
            peer = lax.rem(me + k, cp)
            link(kind, src.at[which(peer)], dst.at[me], peer, peer, me).start()

        dst[me] = src[which(me)]

    def spread_sent(kind, src, dst, which):
        @pl.loop(1, cp)
        def _(k):
            peer = lax.rem(me + k, cp)
            link(kind, src.at[which(peer)], dst.at[me], peer, peer, me).wait_send()

    def spread_arrive(kind, src, dst):
        @pl.loop(1, cp)
        def _(k):
            peer = lax.rem(me + k, cp)
            link(kind, src.at[0], dst.at[peer], peer, peer, peer).wait_recv()

    def one_out(kind, src, dst, i):
        @pl.when(me != i)
        def _():
            link(kind, src.at[i], dst.at[me], i, i, me).start()

        @pl.when(me == i)
        def _():
            dst[me] = src[i]

    def one_sent(kind, src, dst, i):
        @pl.when(me != i)
        def _():
            link(kind, src.at[i], dst.at[me], i, i, me).wait_send()

    def when_mine(i, body):
        if share == 1:
            body()
        else:
            pl.when(mine == i % share)(body)

    def source(h):
        return h * share + lax.rem(me, share)

    def from_heads(kind, dst, src):
        for h in range(heads):
            peer = source(h)

            @pl.when(peer != me)
            def _():
                link(kind, src.at[0], dst.at[peer], peer, peer, peer).wait_recv()

    owner = own_col[...]
    place = owner * capacity + ranks_column(owner, devices)
    chosen = (place == iota((rows, slots), 1)).astype(F32).astype(BF16)
    for t in range(devices):
        slots_f32[t * capacity : (t + 1) * capacity, :] = got[t].astype(F32)
    lane_of = (ranks_column(owner, devices) == iota((rows, LANES), 1)).astype(F32)
    match = (owner == iota((rows, devices), 1)).astype(F32)
    scale = jnp.sum(dot_f32(match, got_scale[:, 0, :]) * lane_of, axis=1, keepdims=True)
    emb = dot(chosen, slots_f32[...].astype(BF16)) * scale
    embedded[...] = emb
    norm, inv_embed = normalize(emb)
    normed[...] = norm
    norm16 = norm.astype(BF16)
    load_in.wait()
    head_of = lambda peer: lax.div(peer, share)
    for kind, group, snd, full in ((0, 3, snd_k, all_k), (1, 2, snd_q, all_q), (2, 1, snd_v, all_v)):
        part = dot(norm16, win[:, group * width : (group + 1) * width])
        projected[:, group * width : (group + 1) * width] = part
        act = (part * jax.nn.sigmoid(part)).astype(BF16)
        for h in range(heads):
            snd[h] = act[:, h * hd : (h + 1) * hd]
        spread(kind, snd, full, head_of)
    part = dot(norm16, win[:, :width])
    projected[:, :width] = part
    gate_s[...] = (part * jax.nn.sigmoid(part)).astype(BF16).astype(F32)
    load_out.wait()
    gm_s[...] = dot_nt(cot_ref[...], wout[...])
    spread_arrive(0, snd_k, all_k)
    spread_arrive(1, snd_q, all_q)
    spread_arrive(2, snd_v, all_v)

    scaling = hd ** (-0.5)
    documents = lengths.shape[1]
    for i in range(cp):

        def forward(i=i):
            extent = (i + 1) * rows
            keys = all_k[: i + 1].reshape(extent, hd)
            s = dot_nt(all_q[i], keys) * scaling
            pos = i * rows + iota((rows, 1), 0)
            first = jnp.zeros((rows, 1), jnp.int32)
            count = jnp.ones((rows, 1), jnp.int32)
            begin = 0
            for d in range(documents):
                size = lengths[0, d]
                inside = (pos >= begin) & (pos < begin + size)
                first = jnp.where(inside, begin, first)
                count = jnp.where(inside, size, count)
                begin = begin + size
            inverse = 1.0 / count.astype(F32)
            key_pos = iota((rows, extent), 1)
            allowed = (key_pos >= first) & (key_pos <= pos)
            sig = jax.nn.sigmoid(s)
            a = jnp.where(allowed, s * sig * inverse, 0.0).astype(BF16)
            weights[i * rows : (i + 1) * rows, :extent] = a
            slope[i * rows : (i + 1) * rows, :extent] = jnp.where(
                allowed, sig * (1.0 + s * (1.0 - sig)) * (inverse * scaling), 0.0
            )
            snd_att[i] = dot(a, all_v[: i + 1].reshape(extent, hd)).astype(BF16)
            one_out(3, snd_att, all_att, i)

        when_mine(i, forward)

    from_heads(3, all_att, snd_att)
    for h in range(heads):
        flat[:, h * hd : (h + 1) * hd] = all_att[source(h)].astype(F32)
    attn_norm, inv_attn = normalize(flat[...])
    flat[...] = attn_norm
    gm = gm_s[...]
    gate = gate_s[...]
    ga = normalize_back(gm * gate, attn_norm, inv_attn).astype(BF16)
    for h in range(heads):
        snd_ga[h] = ga[:, h * hd : (h + 1) * hd]
    for h in range(heads):
        peer = source(h)

        @pl.when(peer != me)
        def _():
            link(4, snd_ga.at[h], all_ga.at[me], peer, h, me).start()

        @pl.when(peer == me)
        def _():
            all_ga[me] = snd_ga[h]

    def silu_slope(v):
        sig = jax.nn.sigmoid(v)
        return sig * (1.0 + v * (1.0 - sig))

    mixed = (attn_norm * gate).astype(BF16)
    layer_out[...] = (embedded[...] + dot(mixed, wout[...])).astype(BF16)
    grad_u = (gm * attn_norm * silu_slope(projected[:, :width])).astype(BF16)
    gm_s[...] = dot_nt(grad_u, win[:, :width])
    for g in range(1, 4):
        gp_s[:, g * width : (g + 1) * width] = silu_slope(projected[:, g * width : (g + 1) * width])

    dk_sum[...] = jnp.zeros_like(dk_sum)
    dv_sum[...] = jnp.zeros_like(dv_sum)
    for i in reversed(range(cp)):

        def backward(i=i):
            extent = (i + 1) * rows

            @pl.when(me != i)
            def _():
                link(4, snd_ga.at[0], all_ga.at[i], i, 0, i).wait_recv()

            grad = all_ga[i]
            grad_a = dot_nt(grad, all_v[: i + 1].reshape(extent, hd))
            grad_s = (grad_a * slope[i * rows : (i + 1) * rows, :extent]).astype(BF16)
            snd_dq[i] = dot(grad_s, all_k[: i + 1].reshape(extent, hd)).astype(BF16)
            one_out(5, snd_dq, all_dq, i)
            dk_sum[:extent, :] += dot_tn(grad_s, all_q[i])
            dv_sum[:extent, :] += dot_tn(weights[i * rows : (i + 1) * rows, :extent], grad)

        when_mine(i, backward)
        snd_dk[i] = dk_sum[i * rows : (i + 1) * rows, :].astype(BF16)
        one_out(6, snd_dk, all_dk, i)
        snd_dv[i] = dv_sum[i * rows : (i + 1) * rows, :].astype(BF16)
        one_out(7, snd_dv, all_dv, i)

    from_heads(5, all_dq, snd_dq)

    def finish(group, whole, take):
        for h in range(heads):
            at = slice(group * width + h * hd, group * width + (h + 1) * hd)
            whole[:, at] = (take(h) * whole[:, at])

    finish(2, gp_s, lambda h: all_dq[source(h)].astype(F32))
    grad_norm = gm_s[...] + dot_nt(
        gp_s[:, 2 * width : 3 * width].astype(BF16), win[:, 2 * width : 3 * width]
    )
    for kind, group, snd, full in ((6, 3, snd_dk, all_dk), (7, 1, snd_dv, all_dv)):
        spread_arrive(kind, snd, full)

        def summed(h, full=full):
            total = full[h * share].astype(F32)
            for r in range(1, share):
                total = total + full[h * share + r].astype(F32)
            return total

        finish(group, gp_s, summed)
        grad_norm = grad_norm + dot_nt(
            gp_s[:, group * width : (group + 1) * width].astype(BF16),
            win[:, group * width : (group + 1) * width],
        )
    grad_embed = cot_ref[...].astype(F32) + normalize_back(grad_norm, normed[...], inv_embed)
    owner_row = own_row[...]
    place_row = owner_row * capacity + ranks_row(owner_row, devices)
    back = (place_row == iota((slots, rows), 0)).astype(F32).astype(BF16)
    leaving = dot(back, grad_embed.astype(BF16))
    for t in range(devices):
        outgoing[t] = leaving[t * capacity : (t + 1) * capacity, :].astype(BF16)

    for kind, snd, full in ((0, snd_k, all_k), (1, snd_q, all_q), (2, snd_v, all_v)):
        spread_sent(kind, snd, full, head_of)
    for i in range(cp):

        def drained(i=i):
            one_sent(3, snd_att, all_att, i)
            one_sent(5, snd_dq, all_dq, i)

        when_mine(i, drained)
        one_sent(6, snd_dk, all_dk, i)
        one_sent(7, snd_dv, all_dv, i)
    for h in range(heads):
        peer = source(h)

        @pl.when(peer != me)
        def _():
            link(4, snd_ga.at[h], all_ga.at[me], peer, h, me).wait_send()


def return_kernel(devices, src, dst, send_sem, recv_sem, local_sem):
    me = flat_index()
    own = pltpu.make_async_copy(src.at[me], dst.at[me], local_sem)
    own.start()
    greet(me, devices, flat_id)

    def link(peer, at, sem):
        return pltpu.make_async_remote_copy(
            src_ref=src.at[peer],
            dst_ref=dst.at[at],
            send_sem=send_sem.at[peer],
            recv_sem=recv_sem.at[sem],
            device_id=flat_id(peer),
            device_id_type=MESH,
        )

    @pl.loop(1, devices)
    def _(k):
        link(lax.rem(me + k, devices), me, me).start()

    own.wait()

    @pl.loop(1, devices)
    def _(k):
        peer = lax.rem(me + k, devices)
        link(peer, peer, peer).wait_recv()

    @pl.loop(1, devices)
    def _(k):
        link(lax.rem(me + k, devices), me, me).wait_send()


def table_kernel(tile, slots, capacity, lookup, arrived, scale_ref, out):
    base = pl.program_id(0) * tile
    wide = lookup[...] - 1 - base
    one_hot = (wide == iota((tile, slots), 0)).astype(F32).astype(BF16)
    total = dot(one_hot, arrived[...])
    eye = (iota((LANES, LANES), 0) == iota((LANES, LANES), 1)).astype(F32)
    for b in range(tile // LANES):
        column = jnp.sum(eye * scale_ref[b], axis=1, keepdims=True)
        out[b * LANES : (b + 1) * LANES, :] = total[b * LANES : (b + 1) * LANES, :] * column


def per_device(
    table_rows,
    row_scales,
    owners,
    shard_rows,
    history_lengths,
    input_weight,
    output_weight,
    cotangent,
):
    rows = owners.shape[0]
    table_size, width = table_rows.shape
    devices = lax.axis_size(("dp", "cp"))
    cp = lax.axis_size("cp")
    capacity = max(2, 2 * rows // devices)
    slots = devices * capacity
    hd = width // HEADS
    vmem = pl.BlockSpec(memory_space=pltpu.VMEM)
    smem = pl.BlockSpec(memory_space=pltpu.SMEM)
    anywhere = pl.BlockSpec(memory_space=pl.ANY)
    owner_row = owners.reshape(1, rows)
    scale_lines = row_scales.reshape(table_size // LANES, LANES)

    def params(number):
        return pltpu.CompilerParams(
            collective_id=number, has_side_effects=True, vmem_limit_bytes=VMEM_LIMIT
        )

    incoming, got, got_scale = pl.pallas_call(
        functools.partial(fetch_kernel, devices, capacity),
        out_shape=(
            jax.ShapeDtypeStruct((devices, 1, LANES), jnp.int32),
            jax.ShapeDtypeStruct((devices, capacity, width), BF16),
            jax.ShapeDtypeStruct((devices, 1, LANES), F32),
        ),
        in_specs=[vmem, vmem, vmem, anywhere, vmem],
        out_specs=(vmem, vmem, vmem),
        scratch_shapes=[
            pltpu.VMEM((devices, 1, LANES), jnp.int32),
            pltpu.VMEM((table_size, width), BF16),
            pltpu.VMEM((devices, capacity, width), BF16),
            pltpu.VMEM((devices, 1, LANES), F32),
            pltpu.SemaphoreType.DMA((3, devices)),
            pltpu.SemaphoreType.DMA((3, devices)),
            pltpu.SemaphoreType.DMA((1,)),
        ],
        compiler_params=params(0),
    )(owners, owner_row, shard_rows.reshape(rows, 1), table_rows, scale_lines)

    line = cp * rows
    full = lambda: pltpu.VMEM((cp, rows, hd), BF16)
    by_head = lambda: pltpu.VMEM((HEADS, rows, hd), BF16)
    layer_out, outgoing = pl.pallas_call(
        functools.partial(layer_kernel, devices, capacity, cp),
        out_shape=(
            jax.ShapeDtypeStruct((rows, width), BF16),
            jax.ShapeDtypeStruct((devices, capacity, width), BF16),
        ),
        in_specs=[smem, vmem, vmem, vmem, vmem, anywhere, anywhere, vmem],
        out_specs=(vmem, vmem),
        scratch_shapes=[
            pltpu.VMEM(input_weight.shape, BF16),
            pltpu.VMEM(output_weight.shape, BF16),
            pltpu.VMEM((rows, width), F32),
            pltpu.VMEM((slots, width), F32),
            pltpu.VMEM((rows, 4 * width), F32),
            pltpu.VMEM((rows, width), F32),
            pltpu.VMEM((rows, width), F32),
            pltpu.VMEM((rows, width), F32),
            pltpu.VMEM((rows, width), F32),
            by_head(), by_head(), by_head(), full(), full(), full(),
            full(), full(), by_head(), full(), full(), full(), full(), full(), full(), full(),
            pltpu.VMEM((line, line), BF16),
            pltpu.VMEM((line, line), F32),
            pltpu.VMEM((line, hd), F32),
            pltpu.VMEM((line, hd), F32),
            pltpu.VMEM((rows, 4 * width), F32),
            pltpu.SemaphoreType.DMA((8, cp)),
            pltpu.SemaphoreType.DMA((8, cp)),
            pltpu.SemaphoreType.DMA((2,)),
        ],
        compiler_params=params(1),
    )(history_lengths, owners, owner_row, got, got_scale, input_weight, output_weight, cotangent)

    arrived = pl.pallas_call(
        functools.partial(return_kernel, devices),
        out_shape=jax.ShapeDtypeStruct((devices, capacity, width), BF16),
        in_specs=[vmem],
        out_specs=vmem,
        scratch_shapes=[
            pltpu.SemaphoreType.DMA((devices,)),
            pltpu.SemaphoreType.DMA((devices,)),
            pltpu.SemaphoreType.DMA(()),
        ],
        compiler_params=params(2),
    )(outgoing)

    tile = min(256, table_size)
    lookup = incoming[:, 0, :capacity].reshape(1, slots)
    table_grad = pl.pallas_call(
        functools.partial(table_kernel, tile, slots, capacity),
        out_shape=jax.ShapeDtypeStruct((table_size, width), F32),
        grid=(table_size // tile,),
        in_specs=[
            pl.BlockSpec((1, slots), lambda b: (0, 0)),
            pl.BlockSpec((slots, width), lambda b: (0, 0)),
            pl.BlockSpec((tile // LANES, 1, LANES), lambda b: (b, 0, 0)),
        ],
        out_specs=pl.BlockSpec((tile, width), lambda b: (b, 0)),
        compiler_params=pltpu.CompilerParams(vmem_limit_bytes=VMEM_LIMIT // 2),
    )(lookup, arrived.reshape(slots, width), row_scales.reshape(table_size // LANES, 1, LANES))
    return (layer_out, table_grad)


def solution(mesh):
    return jax.shard_map(
        per_device,
        mesh=mesh,
        in_specs=(
            P(("dp", "cp"), None),
            P(("dp", "cp")),
            P(("dp", "cp"), None),
            P(("dp", "cp")),
            P("dp", None),
            P(),
            P(),
            P(("dp", "cp"), None),
        ),
        out_specs=(P(("dp", "cp"), None), P(("dp", "cp"), None)),
        check_vma=False,
    )
```

time: 271 us -> 105 us (0.39); the launches traced: 266 us -> 105 us
  waiting for transfers between devices: 119 us -> 0 us
  Pallas kernels: 0 us -> 99 us
  matrix products: 51.6 us -> 0 us
  other arithmetic: 32.4 us -> 0 us
  local copies, waits for them, and re-layouts: 27.2 us -> 5.37 us
  between operations: 15.2 us -> 0.68 us
  blocking collectives: 10.8 us -> 0 us
  starting transfers between devices: 10.1 us -> 0 us
    pallas_call x0 -> x4, Pallas kernels: none -> 99 us  [the longest x1 42.9 us: per_device(): pl.pallas_call(functools.partial(layer_kernel, devices, capacity, cp), ou...]
    all_gather x4 -> x0, waiting for transfers between devices: 72.3 us -> none  [the longest x1 29.8 us: per_device(): lax.all_gather(key_rows, 'cp', axis=0, tiled=True)]
    dot_general x10 -> x0, matrix products: 51.6 us -> none  [the longest x1 8.38 us: per_device(): jnp.einsum('rk,dk->rd', grad_proj, input_weight, preferred_element_type=j...]
    all_to_all x2 -> x0, waiting for transfers between devices: 45.1 us -> none  [the longest x1 23.7 us: per_device(): lax.all_to_all(fetched.reshape(devices, capacity, model_width), ('dp', 'c...]
    all_to_all x1 -> x0, blocking collectives: 10.8 us -> none  [per_device(): lax.all_to_all(requests.reshape(devices, capacity), ('dp', 'cp'), split_a...]
    all_to_all x2 -> x0, starting transfers between devices: 9.95 us -> none  [the longest x1 5.02 us: per_device(): lax.all_to_all(fetched.reshape(devices, capacity, model_width), ('dp', 'c...]
    mul x2 -> x0, other arithmetic: 9.47 us -> none  [the longest x1 7.39 us: per_device(): table_grad = summed * row_scales[:, None]]
    gather x3 -> x0, local copies, waits for them, and re-layouts: 7.81 us -> none  [the longest x1 4.3 us: per_device(): table_rows[lookup].astype(jnp.float32) * row_scales[lookup][:, None]]
  transfers between devices with their start and end apart: 6 -> 0, of which waited for: 5 -> 0; matrix products, arithmetic and copies ran while one was open for 17% -> 0% of each run, Pallas kernels for 0% -> 0%
where the time goes in v1:
time: 105 us
  Pallas kernels  99 us (94%)
  local copies, waits for them, and re-layouts  5.37 us (5%)
    pallas_call x1, Pallas kernels, per_device(): pl.pallas_call(functools.partial(layer_kernel, devices, capacity, cp), ou...  42.9 us
    pallas_call x1, Pallas kernels, per_device(): pl.pallas_call(functools.partial(fetch_kernel, devices, capacity), out_sh...  29.5 us
    pallas_call x1, Pallas kernels, per_device(): pl.pallas_call(functools.partial(return_kernel, devices), out_shape=jax.S...  21.1 us
    pallas_call x1, Pallas kernels, per_device(): pl.pallas_call(functools.partial(table_kernel, tile, slots, capacity), ou...  5.45 us
    unnamed x8, local copies, waits for them, and re-layouts  3.14 us

profile of v1, /device:TPU:13, one launch (start us, length us, event | category | flops | bytes accessed | tf_op | source)
XLA Modules:
  0.0 105.0 jit_solution(2065764041823491078)
XLA Ops:
  0.6 1.4 %copy.15.own_col = s32[128,1]{1,0:T(8,128)} copy(s32[128,1]{0,1:T(1,128)} %param.10) | data formatting | bytes 1024 | tf_op args[2]
  2.0 1.4 %copy.14.row_col = s32[128,1]{1,0:T(8,128)} copy(s32[128,1]{0,1:T(1,128)} %bitcast.10) | data formatting | bytes 1024 | tf_op jit(solution)/shard_map/reshape | solution.py:517
  3.4 0.0 copy-start.1
  3.4 29.5 %shard_map.95 = (s32[32,1,128]{2,1,0:T(1,128)}, bf16[32,8,1024]{2,1,0:T(8,128)(2,1)}, f32[32,1,128]{2,1,0:T(1,128)}) custom-call(s32[128,1]{1,0:T(8,128)} %copy.15.own_col, s32[1,128]{1,0:T(1,128)} %bitcast.8, s32[128,1]{1,0:T(8,128)} %copy.14.row_col, bf16[2048,1024]{1,0:T(8,128)(2,1)} %table_any.1, f32[16,128]{1,0:T(8,128)} %bitcast.6), custom_call_target="tpu_custom_call" | custom-call | tf_op jit(solution)/shard_map/pallas_call | solution.py:498
  32.9 0.8 slice_reduce_fusion
  33.7 0.1 reshape_squeeze.3.lookup
  33.8 42.9 %shard_map.96 = (bf16[128,1024]{1,0:T(8,128)(2,1)}, bf16[32,8,1024]{2,1,0:T(8,128)(2,1)}) custom-call(s32[1,3]{1,0:T(1,128)} %lengths.1, s32[128,1]{1,0:T(8,128)} %copy.15.own_col, s32[1,128]{1,0:T(1,128)} %bitcast.9, bf16[32,8,1024]{2,1,0:T(8,128)(2,1)} %get-tuple-element.7.got, f32[32,1,128]{2,1,0:T(1,128)} %get-tuple-element.8.got_scale, ...), custom_call_target="tpu_custom_call" | custom-call | tf_op jit(solution)/shard_map/pallas_call | solution.py:522
  76.7 0.0 copy-start.2
  76.7 21.1 %shard_map.97 = bf16[32,8,1024]{2,1,0:T(8,128)(2,1)} custom-call(bf16[32,8,1024]{2,1,0:T(8,128)(2,1)} %get-tuple-element.11.src), custom_call_target="tpu_custom_call" | custom-call | tf_op jit(solution)/shard_map/pallas_call | solution.py:554
  97.8 0.0 copy-done.1
  97.8 0.0 copy-start
  97.9 1.0 copy-done
  98.9 5.5 %shard_map.98 = f32[2048,1024]{1,0:T(8,128)} custom-call(s32[1,256]{1,0:T(1,128)S(1)} %reshape_squeeze.3.lookup, bf16[256,1024]{1,0:T(8,128)(2,1)S(1)} %bitcast.5, f32[16,1,128]{2,1,0:T(1,128)S(1)} %bitcast.7), custom_call_target="tpu_custom_call" | custom-call | tf_op jit(solution)/shard_map/pallas_call | solution.py:569
  104.3 0.0 copy-done.2
  104.3 0.7 copy.17
Async XLA Ops:
  3.4 94.4 %copy-start.1 = (f32[2048]{0:T(1024)S(1)}, f32[2048]{0:T(1024)}, u32[]{:S(2)}) copy-start(f32[2048]{0:T(1024)} %param.9) | copy-start | bytes 24580
  76.7 27.7 %copy-start.2 = (bf16[128,1024]{1,0:T(8,128)(2,1)S(1)}, bf16[128,1024]{1,0:T(8,128)(2,1)}, u32[]{:S(2)}) copy-start(bf16[128,1024]{1,0:T(8,128)(2,1)} %get-tuple-element.14) | copy-start | bytes 786436
  97.8 1.0 copy-start

commit v2 on v1

v2 whole, which is shorter than its diff:
```python
import functools

import jax
import jax.numpy as jnp
from jax import lax
from jax.experimental import pallas as pl
from jax.experimental.pallas import tpu as pltpu
from jax.sharding import PartitionSpec as P

HEADS = 8
EPSILON = 1e-05
LANES = 128
MESH = pl.DeviceIdType.MESH
EXACT = lax.Precision.HIGHEST
F32 = jnp.float32
BF16 = jnp.bfloat16
VMEM_LIMIT = 60 * 1024 * 1024


def iota(shape, axis):
    return lax.broadcasted_iota(jnp.int32, shape, axis)


def dot_f32(a, b):
    return jnp.dot(a, b, precision=EXACT, preferred_element_type=F32)


def dot(a, b):
    return jnp.dot(a, b, preferred_element_type=F32)


def dot_nt(a, b):
    return lax.dot_general(a, b, (((1,), (1,)), ((), ())), preferred_element_type=F32)


def dot_tn(a, b):
    return lax.dot_general(a, b, (((0,), (0,)), ((), ())), preferred_element_type=F32)


def normalize(values):
    center = jnp.mean(values, axis=-1, keepdims=True)
    shifted = values - center
    inv_spread = lax.rsqrt(jnp.mean(shifted * shifted, axis=-1, keepdims=True) + EPSILON)
    return shifted * inv_spread, inv_spread


def normalize_back(grad_in, normed, inv_spread):
    return inv_spread * (
        grad_in
        - jnp.mean(grad_in, axis=-1, keepdims=True)
        - normed * jnp.mean(grad_in * normed, axis=-1, keepdims=True)
    )


def ranks_column(owner_col, devices):
    rows = owner_col.shape[0]
    match = (owner_col == iota((rows, devices), 1)).astype(F32)
    earlier = (iota((rows, rows), 1) < iota((rows, rows), 0)).astype(BF16)
    before = dot(earlier, match.astype(BF16))
    return jnp.sum(before * match, axis=1, keepdims=True).astype(jnp.int32)


def ranks_row(owner_row, devices):
    rows = owner_row.shape[1]
    match = (owner_row == iota((devices, rows), 0)).astype(F32)
    earlier = (iota((rows, rows), 0) < iota((rows, rows), 1)).astype(BF16)
    before = dot(match.astype(BF16), earlier)
    return jnp.sum(before * match, axis=0, keepdims=True).astype(jnp.int32)


def flat_index():
    return lax.axis_index("dp") * lax.axis_size("cp") + lax.axis_index("cp")


def flat_id(peer):
    size = lax.axis_size("cp")
    return {"dp": lax.div(peer, size), "cp": lax.rem(peer, size)}


def column_of(row):
    size = row.shape[1]
    eye = (iota((size, size), 0) == iota((size, size), 1)).astype(F32)
    return (jnp.sum(eye * row.astype(F32), axis=1, keepdims=True) + 0.5).astype(jnp.int32)


def sigmoid(v):
    return 0.5 * jnp.tanh(0.5 * v) + 0.5


def silu_slope(v):
    sig = sigmoid(v)
    return sig * (1.0 + v * (1.0 - sig))


def layer_kernel(
    devices, capacity, cp, lengths, own_row, row_row, scale_ref, cot_ref, table_any, win_any, wout_any,
    layer_out, lookup, arrived,
    request, incoming, table, rows_out, scale_out, got, got_scale, outgoing,
    win, wout, flat, slots_f32, projected, embedded, normed, gate_s, gm_s,
    snd_k, snd_v, snd_q, all_k, all_v, all_q,
    snd_att, all_att, snd_ga, all_ga, snd_dq, snd_dk, snd_dv, all_dq, all_dk, all_dv,
    weights, slope, dk_sum, dv_sum,
    wide_send, wide_recv, send_sem, recv_sem, local_sem,
):
    whole_me = flat_index()
    me = lax.axis_index("cp")
    rows, width = layer_out.shape
    heads = HEADS
    hd = width // heads
    share = cp // heads
    slots = devices * capacity
    mine = lax.rem(me, share)
    pair = 2 if cp % (2 * share) == 0 else 1
    span = pair * rows
    loads = [
        pltpu.make_async_copy(table_any, table, local_sem.at[0]),
        pltpu.make_async_copy(wout_any, wout, local_sem.at[1]),
        pltpu.make_async_copy(win_any, win, local_sem.at[2]),
    ]
    barrier = pltpu.get_barrier_semaphore()

    @pl.loop(1, devices)
    def _(k):
        pl.semaphore_signal(
            barrier,
            inc=1,
            device_id=flat_id(lax.rem(whole_me + k, devices)),
            device_id_type=MESH,
        )

    for load in loads:
        load.start()

    def wide(kind, src, dst, peer, at, sem):
        return pltpu.make_async_remote_copy(
            src_ref=src.at[peer],
            dst_ref=dst.at[at],
            send_sem=wide_send.at[kind, peer],
            recv_sem=wide_recv.at[kind, sem],
            device_id=flat_id(peer),
            device_id_type=MESH,
        )

    def wide_start(kind, src, dst):
        @pl.loop(1, devices)
        def _(k):
            wide(kind, src, dst, lax.rem(whole_me + k, devices), whole_me, whole_me).start()

        dst[whole_me] = src[whole_me]

    def wide_arrive(kind, src, dst):
        @pl.loop(1, devices)
        def _(k):
            peer = lax.rem(whole_me + k, devices)
            wide(kind, src, dst, peer, peer, peer).wait_recv()

    def wide_sent(kind, src, dst):
        @pl.loop(1, devices)
        def _(k):
            wide(kind, src, dst, lax.rem(whole_me + k, devices), whole_me, whole_me).wait_send()

    def link(kind, src, dst, peer, send_at, recv_at):
        return pltpu.make_async_remote_copy(
            src_ref=src,
            dst_ref=dst,
            send_sem=send_sem.at[kind, send_at],
            recv_sem=recv_sem.at[kind, recv_at],
            device_id={"cp": peer},
            device_id_type=MESH,
        )

    def spread(kind, src, dst, which):
        @pl.loop(1, cp)
        def _(k):
            peer = lax.rem(me + k, cp)
            link(kind, src.at[which(peer)], dst.at[me], peer, peer, me).start()

        dst[me] = src[which(me)]

    def spread_sent(kind, src, dst, which):
        @pl.loop(1, cp)
        def _(k):
            peer = lax.rem(me + k, cp)
            link(kind, src.at[which(peer)], dst.at[me], peer, peer, me).wait_send()

    def spread_arrive(kind, src, dst):
        @pl.loop(1, cp)
        def _(k):
            peer = lax.rem(me + k, cp)
            link(kind, src.at[0], dst.at[peer], peer, peer, peer).wait_recv()

    def one_out(kind, src, dst, i):
        @pl.when(me != i)
        def _():
            link(kind, src.at[i], dst.at[me], i, i, me).start()

        @pl.when(me == i)
        def _():
            dst[me] = src[i]

    def one_sent(kind, src, dst, i):
        @pl.when(me != i)
        def _():
            link(kind, src.at[i], dst.at[me], i, i, me).wait_send()

    def when_mine(i, body):
        if share == 1:
            body()
        else:
            pl.when(mine == i % share)(body)

    def source(h):
        return h * share + lax.rem(lax.div(me, pair), share)

    def from_heads(kind, dst, src):
        for h in range(heads):
            peer = source(h)

            @pl.when(peer != me)
            def _():
                link(kind, src.at[0], dst.at[peer], peer, peer, peer).wait_recv()

    owner_row = own_row[...]
    owner = column_of(owner_row)
    row_index = column_of(row_row[...])
    rank = ranks_column(owner, devices)
    spots = (rank == iota((rows, LANES), 1)).astype(F32)
    named = (owner_row == iota((devices, rows), 0)).astype(F32)
    wanted = (dot_f32(named, spots * (row_index + 1).astype(F32)) + 0.5).astype(jnp.int32)
    for t in range(devices):
        request[t] = wanted[t : t + 1, :]
    pl.semaphore_wait(barrier, devices - 1)
    wide_start(0, request, incoming)
    loads[1].wait()
    gm_s[...] = dot_nt(cot_ref[...], wout[...])
    loads[0].wait()
    wide_arrive(0, request, incoming)

    asked = incoming[:, 0, :].astype(F32)
    of_slot = (lax.div(iota((slots, devices), 0), capacity) == iota((slots, devices), 1)).astype(F32)
    lane_of = (lax.rem(iota((slots, LANES), 0), capacity) == iota((slots, LANES), 1)).astype(F32)
    index = (jnp.sum(dot_f32(of_slot, asked) * lane_of, axis=1, keepdims=True) + 0.5).astype(
        jnp.int32
    ) - 1
    total = table.shape[0]
    one_hot = (index == iota((slots, total), 1)).astype(F32).astype(BF16)
    values = dot(one_hot, table[...])
    for t in range(devices):
        rows_out[t] = values[t * capacity : (t + 1) * capacity, :].astype(BF16)
    wide_start(2, rows_out, got)
    groups = total // LANES
    high = (lax.shift_right_arithmetic(index, 7) == iota((slots, groups), 1)).astype(F32)
    low = ((index & (LANES - 1)) == iota((slots, LANES), 1)).astype(F32)
    picked = jnp.sum(dot_f32(high, scale_ref[...]) * low, axis=1, keepdims=True)
    to_device = (
        lax.div(iota((devices, slots), 1), capacity) == iota((devices, slots), 0)
    ).astype(F32)
    scales = dot_f32(to_device, picked * lane_of)
    for t in range(devices):
        scale_out[t] = scales[t : t + 1, :]
    wide_start(1, scale_out, got_scale)
    lane_col = (lax.rem(iota((LANES, slots), 1), capacity) == iota((LANES, slots), 0)).astype(F32)
    line_up = jnp.sum(dot_f32(asked, lane_col) * to_device, axis=0, keepdims=True)
    lookup[...] = (line_up + 0.5).astype(jnp.int32) - 1
    place = owner * capacity + rank
    chosen = (place == iota((rows, slots), 1)).astype(F32).astype(BF16)
    match = (owner == iota((rows, devices), 1)).astype(F32)
    loads[2].wait()
    wide_arrive(1, scale_out, got_scale)
    scale = jnp.sum(dot_f32(match, got_scale[:, 0, :]) * spots, axis=1, keepdims=True)
    wide_arrive(2, rows_out, got)
    for t in range(devices):
        slots_f32[t * capacity : (t + 1) * capacity, :] = got[t].astype(F32)
    emb = dot(chosen, slots_f32[...].astype(BF16)) * scale
    embedded[...] = emb
    norm, inv_embed = normalize(emb)
    normed[...] = norm
    norm16 = norm.astype(BF16)
    head_of = lambda peer: lax.div(peer, share)
    for kind, group, snd, full in ((0, 3, snd_k, all_k), (1, 2, snd_q, all_q), (2, 1, snd_v, all_v)):
        part = dot(norm16, win[:, group * width : (group + 1) * width])
        projected[:, group * width : (group + 1) * width] = part
        act = (part * sigmoid(part)).astype(BF16)
        for h in range(heads):
            snd[h] = act[:, h * hd : (h + 1) * hd]
        spread(kind, snd, full, head_of)
    part = dot(norm16, win[:, :width])
    gate_s[...] = (part * sigmoid(part)).astype(BF16).astype(F32)
    projected[:, :width] = silu_slope(part)
    for g in range(1, 4):
        at = slice(g * width, (g + 1) * width)
        projected[:, at] = silu_slope(projected[:, at])
    dk_sum[...] = jnp.zeros_like(dk_sum)
    dv_sum[...] = jnp.zeros_like(dv_sum)

    scaling = hd ** (-0.5)
    documents = lengths.shape[1]
    for g in range(cp // pair):
        members = range(g * pair, (g + 1) * pair)
        for i in members:

            @pl.when(me != i)
            def _():
                for kind, snd, full in ((0, snd_k, all_k), (1, snd_q, all_q), (2, snd_v, all_v)):
                    link(kind, snd.at[0], full.at[i], i, i, i).wait_recv()

        def forward(g=g, members=members):
            extent = (g + 1) * span
            here = slice(g * span, (g + 1) * span)
            upto = (g + 1) * pair
            keys = all_k[:upto].reshape(extent, hd)
            s = dot_nt(all_q[g * pair : upto].reshape(span, hd), keys) * scaling
            pos = g * span + iota((span, 1), 0)
            first = jnp.zeros((span, 1), jnp.int32)
            count = jnp.ones((span, 1), jnp.int32)
            begin = 0
            for d in range(documents):
                size = lengths[0, d]
                inside = (pos >= begin) & (pos < begin + size)
                first = jnp.where(inside, begin, first)
                count = jnp.where(inside, size, count)
                begin = begin + size
            inverse = 1.0 / count.astype(F32)
            key_pos = iota((span, extent), 1)
            allowed = (key_pos >= first) & (key_pos <= pos)
            sig = sigmoid(s)
            a = jnp.where(allowed, s * sig * inverse, 0.0).astype(BF16)
            weights[here, :extent] = a
            slope[here, :extent] = jnp.where(
                allowed, sig * (1.0 + s * (1.0 - sig)) * (inverse * scaling), 0.0
            )
            result = dot(a, all_v[:upto].reshape(extent, hd)).astype(BF16)
            for j, i in enumerate(members):
                snd_att[i] = result[j * rows : (j + 1) * rows, :]
                one_out(3, snd_att, all_att, i)

        when_mine(g, forward)

    from_heads(3, all_att, snd_att)
    for h in range(heads):
        flat[:, h * hd : (h + 1) * hd] = all_att[source(h)].astype(F32)
    attn_norm, inv_attn = normalize(flat[...])
    flat[...] = attn_norm
    gm = gm_s[...]
    gate = gate_s[...]
    ga = normalize_back(gm * gate, attn_norm, inv_attn).astype(BF16)
    for h in range(heads):
        snd_ga[h] = ga[:, h * hd : (h + 1) * hd]
    for h in range(heads):
        peer = source(h)

        @pl.when(peer != me)
        def _():
            link(4, snd_ga.at[h], all_ga.at[me], peer, h, me).start()

        @pl.when(peer == me)
        def _():
            all_ga[me] = snd_ga[h]

    mixed = (attn_norm * gate).astype(BF16)
    layer_out[...] = (embedded[...] + dot(mixed, wout[...])).astype(BF16)
    grad_u = (gm * attn_norm * projected[:, :width]).astype(BF16)
    gm_s[...] = dot_nt(grad_u, win[:, :width])
    for g in reversed(range(cp // pair)):
        members = range(g * pair, (g + 1) * pair)

        def backward(g=g, members=members):
            extent = (g + 1) * span
            here = slice(g * span, (g + 1) * span)
            upto = (g + 1) * pair
            for i in members:

                @pl.when(me != i)
                def _():
                    link(4, snd_ga.at[0], all_ga.at[i], i, 0, i).wait_recv()

            grad = all_ga[g * pair : upto].reshape(span, hd)
            grad_a = dot_nt(grad, all_v[:upto].reshape(extent, hd))
            grad_s = (grad_a * slope[here, :extent]).astype(BF16)
            result = dot(grad_s, all_k[:upto].reshape(extent, hd)).astype(BF16)
            for j, i in enumerate(members):
                snd_dq[i] = result[j * rows : (j + 1) * rows, :]
                one_out(5, snd_dq, all_dq, i)
            dk_sum[:extent, :] += dot_tn(grad_s, all_q[g * pair : upto].reshape(span, hd))
            dv_sum[:extent, :] += dot_tn(weights[here, :extent], grad)

        when_mine(g, backward)
        for i in members:
            snd_dk[i] = dk_sum[i * rows : (i + 1) * rows, :].astype(BF16)
            one_out(6, snd_dk, all_dk, i)
            snd_dv[i] = dv_sum[i * rows : (i + 1) * rows, :].astype(BF16)
            one_out(7, snd_dv, all_dv, i)

    from_heads(5, all_dq, snd_dq)

    def finish(group, whole, take):
        for h in range(heads):
            at = slice(group * width + h * hd, group * width + (h + 1) * hd)
            whole[:, at] = (take(h) * whole[:, at])

    finish(2, projected, lambda h: all_dq[source(h)].astype(F32))
    grad_norm = gm_s[...] + dot_nt(
        projected[:, 2 * width : 3 * width].astype(BF16), win[:, 2 * width : 3 * width]
    )
    for kind, group, snd, full in ((6, 3, snd_dk, all_dk), (7, 1, snd_dv, all_dv)):
        spread_arrive(kind, snd, full)

        def summed(h, full=full):
            total = full[h * share].astype(F32)
            for r in range(1, share):
                total = total + full[h * share + r].astype(F32)
            return total

        finish(group, projected, summed)
        grad_norm = grad_norm + dot_nt(
            projected[:, group * width : (group + 1) * width].astype(BF16),
            win[:, group * width : (group + 1) * width],
        )
    grad_embed = cot_ref[...].astype(F32) + normalize_back(grad_norm, normed[...], inv_embed)
    place_row = owner_row * capacity + ranks_row(owner_row, devices)
    back = (place_row == iota((slots, rows), 0)).astype(F32).astype(BF16)
    leaving = dot(back, grad_embed.astype(BF16))
    for t in range(devices):
        outgoing[t] = leaving[t * capacity : (t + 1) * capacity, :].astype(BF16)

    wide_start(3, outgoing, arrived)
    for kind, snd, full in ((0, snd_k, all_k), (1, snd_q, all_q), (2, snd_v, all_v)):
        spread_sent(kind, snd, full, head_of)
    for i in range(cp):

        def drained(i=i):
            one_sent(3, snd_att, all_att, i)
            one_sent(5, snd_dq, all_dq, i)

        when_mine(i // pair, drained)
        one_sent(6, snd_dk, all_dk, i)
        one_sent(7, snd_dv, all_dv, i)
    for h in range(heads):
        peer = source(h)

        @pl.when(peer != me)
        def _():
            link(4, snd_ga.at[h], all_ga.at[me], peer, h, me).wait_send()
    wide_sent(0, request, incoming)
    wide_sent(1, scale_out, got_scale)
    wide_sent(2, rows_out, got)
    wide_arrive(3, outgoing, arrived)
    wide_sent(3, outgoing, arrived)


def table_kernel(tile, slots, lookup, arrived, scale_ref, layer_in, out, layer_out):
    layer_out[...] = layer_in[...]
    base = pl.program_id(0) * tile
    wide = lookup[...] - base
    one_hot = (wide == iota((tile, slots), 0)).astype(F32).astype(BF16)
    total = dot(one_hot, arrived[...])
    eye = (iota((LANES, LANES), 0) == iota((LANES, LANES), 1)).astype(F32)
    for b in range(tile // LANES):
        column = jnp.sum(eye * scale_ref[b], axis=1, keepdims=True)
        out[b * LANES : (b + 1) * LANES, :] = total[b * LANES : (b + 1) * LANES, :] * column


def per_device(
    table_rows,
    row_scales,
    owners,
    shard_rows,
    history_lengths,
    input_weight,
    output_weight,
    cotangent,
):
    rows = owners.shape[0]
    table_size, width = table_rows.shape
    devices = lax.axis_size(("dp", "cp"))
    cp = lax.axis_size("cp")
    capacity = max(2, 2 * rows // devices)
    slots = devices * capacity
    hd = width // HEADS
    vmem = pl.BlockSpec(memory_space=pltpu.VMEM)
    smem = pl.BlockSpec(memory_space=pltpu.SMEM)
    anywhere = pl.BlockSpec(memory_space=pl.ANY)
    owner_row = owners.reshape(1, rows)
    scale_lines = row_scales.reshape(table_size // LANES, LANES)

    line = cp * rows
    slot_rows = lambda: pltpu.VMEM((devices, capacity, width), BF16)
    full = lambda: pltpu.VMEM((cp, rows, hd), BF16)
    by_head = lambda: pltpu.VMEM((HEADS, rows, hd), BF16)
    layer_out, lookup, arrived = pl.pallas_call(
        functools.partial(layer_kernel, devices, capacity, cp),
        out_shape=(
            jax.ShapeDtypeStruct((rows, width), BF16),
            jax.ShapeDtypeStruct((1, slots), jnp.int32),
            jax.ShapeDtypeStruct((devices, capacity, width), BF16),
        ),
        in_specs=[smem, vmem, vmem, vmem, vmem, anywhere, anywhere, anywhere],
        out_specs=(vmem, vmem, vmem),
        scratch_shapes=[
            pltpu.VMEM((devices, 1, LANES), jnp.int32),
            pltpu.VMEM((devices, 1, LANES), jnp.int32),
            pltpu.VMEM((table_size, width), BF16),
            slot_rows(),
            pltpu.VMEM((devices, 1, LANES), F32),
            slot_rows(),
            pltpu.VMEM((devices, 1, LANES), F32),
            slot_rows(),
            pltpu.VMEM(input_weight.shape, BF16),
            pltpu.VMEM(output_weight.shape, BF16),
            pltpu.VMEM((rows, width), F32),
            pltpu.VMEM((slots, width), F32),
            pltpu.VMEM((rows, 4 * width), F32),
            pltpu.VMEM((rows, width), F32),
            pltpu.VMEM((rows, width), F32),
            pltpu.VMEM((rows, width), F32),
            pltpu.VMEM((rows, width), F32),
            by_head(), by_head(), by_head(), full(), full(), full(),
            full(), full(), by_head(), full(), full(), full(), full(), full(), full(), full(),
            pltpu.VMEM((line, line), BF16),
            pltpu.VMEM((line, line), F32),
            pltpu.VMEM((line, hd), F32),
            pltpu.VMEM((line, hd), F32),
            pltpu.SemaphoreType.DMA((4, devices)),
            pltpu.SemaphoreType.DMA((4, devices)),
            pltpu.SemaphoreType.DMA((8, cp)),
            pltpu.SemaphoreType.DMA((8, cp)),
            pltpu.SemaphoreType.DMA((3,)),
        ],
        compiler_params=pltpu.CompilerParams(
            collective_id=0, has_side_effects=True, vmem_limit_bytes=VMEM_LIMIT
        ),
    )(
        history_lengths,
        owner_row,
        shard_rows.reshape(1, rows),
        scale_lines,
        cotangent,
        table_rows,
        input_weight,
        output_weight,
    )

    tile = min(512, table_size)
    table_grad, layer_out = pl.pallas_call(
        functools.partial(table_kernel, tile, slots),
        out_shape=(
            jax.ShapeDtypeStruct((table_size, width), F32),
            jax.ShapeDtypeStruct((rows, width), BF16),
        ),
        grid=(table_size // tile,),
        in_specs=[
            pl.BlockSpec((1, slots), lambda b: (0, 0)),
            pl.BlockSpec((slots, width), lambda b: (0, 0)),
            pl.BlockSpec((tile // LANES, 1, LANES), lambda b: (b, 0, 0)),
            pl.BlockSpec((rows, width), lambda b: (0, 0)),
        ],
        out_specs=(
            pl.BlockSpec((tile, width), lambda b: (b, 0)),
            pl.BlockSpec((rows, width), lambda b: (0, 0)),
        ),
        compiler_params=pltpu.CompilerParams(vmem_limit_bytes=VMEM_LIMIT),
    )(lookup, arrived.reshape(slots, width), row_scales.reshape(table_size // LANES, 1, LANES), layer_out)
    return (layer_out, table_grad)


def solution(mesh):
    return jax.shard_map(
        per_device,
        mesh=mesh,
        in_specs=(
            P(("dp", "cp"), None),
            P(("dp", "cp")),
            P(("dp", "cp"), None),
            P(("dp", "cp")),
            P("dp", None),
            P(),
            P(),
            P(("dp", "cp"), None),
        ),
        out_specs=(P(("dp", "cp"), None), P(("dp", "cp"), None)),
        check_vma=False,
    )
```

time: 105 us -> 87.1 us (0.83)
  Pallas kernels: 99 us -> 85.9 us
  local copies, waits for them, and re-layouts: 5.37 us -> 0 us
    pallas_call x3 -> x1, Pallas kernels: 56.1 us -> 5.43 us  [per_device(): pl.pallas_call(functools.partial(table_kernel, tile, slots), out_shape=(j...]
    pallas_call x1, Pallas kernels: 42.9 us -> 80.4 us  [per_device(): pl.pallas_call(functools.partial(layer_kernel, devices, capacity, cp), ou...]
    unnamed x8 -> x0, local copies, waits for them, and re-layouts: 3.14 us -> none
    reshape x1 -> x0, local copies, waits for them, and re-layouts: 1.39 us -> none  [per_device(): shard_rows.reshape(rows, 1)]
where the time goes in v2:
time: 87.1 us; the launch traced here: 86.5 us
  Pallas kernels  85.9 us (99%)
    pallas_call x1, Pallas kernels, per_device(): pl.pallas_call(functools.partial(layer_kernel, devices, capacity, cp), ou...  80.4 us
    pallas_call x1, Pallas kernels, per_device(): pl.pallas_call(functools.partial(table_kernel, tile, slots), out_shape=(j...  5.43 us

profile of v2, /device:TPU:13, one launch (start us, length us, event | category | flops | bytes accessed | tf_op | source)
XLA Modules:
  0.0 86.5 jit_solution(7277195941237198917)
XLA Ops:
  0.6 80.4 %shard_map.95 = (bf16[128,1024]{1,0:T(8,128)(2,1)}, s32[1,256]{1,0:T(1,128)}, bf16[32,8,1024]{2,1,0:T(8,128)(2,1)}) custom-call(s32[1,3]{1,0:T(1,128)} %lengths.1, s32[1,128]{1,0:T(1,128)} %bitcast.8, s32[1,128]{1,0:T(1,128)} %bitcast.9, f32[16,128]{1,0:T(8,128)} %bitcast.6, bf16[128,1024]{1,0:T(8,128)(2,1)} %cot_ref.1, bf16[2048,1024]{1,0:T(8,128)(2,1)} %table_any.1, ...), custom_call_target="tpu_custom_call" | custom-call | tf_op jit(solution)/shard_map/pallas_call | solution.py:490
  81.1 5.4 %shard_map.96 = (f32[2048,1024]{1,0:T(8,128)}, bf16[128,1024]{1,0:T(8,128)(2,1)}) custom-call(s32[1,256]{1,0:T(1,128)} %get-tuple-element.7.lookup, bf16[256,1024]{1,0:T(8,128)(2,1)} %bitcast.5, f32[16,1,128]{2,1,0:T(1,128)} %bitcast.7, bf16[128,1024]{1,0:T(8,128)(2,1)} %get-tuple-element.9.layer_in), custom_call_target="tpu_custom_call" | custom-call | tf_op jit(solution)/shard_map/pallas_call | solution.py:544
